TPU v7x, 256 devices: a whole 4x4x8 slice. The times are simulated.
256 devices in a mesh: seq: 64 (over z, x, core), tp: 4 (over y).
Axes of the slice: x: 4, y: 4, z: 8, core: 2. Of those that a mesh axis runs over, the one named last changes fastest.
Arguments:
- tokens: bfloat16 [32768, 4096], P('seq', 'tp'), may hold values from -6 to 6
- log_decay: float32 [32768, 16], P('seq', 'tp'), may hold values from -2 to 0
- w_query: bfloat16 [4096, 2048], P(None, 'tp'), may hold values from -0.09375 to 0.09375
- w_key: bfloat16 [4096, 512], P(None, 'tp'), may hold values from -0.09375 to 0.09375
- w_value: bfloat16 [4096, 512], P(None, 'tp'), may hold values from -0.09375 to 0.09375
- w_level: bfloat16 [4096, 144], P(None, 'tp'), may hold values from -0.09375 to 0.09375
- w_out: bfloat16 [2048, 4096], P('tp'), may hold values from -0.125 to 0.125
Outputs:
- mixed: bfloat16 [32768, 4096], P('seq', 'tp')
All inputs are finite; a program needn't handle non-finite values.
Results may differ from a plain program's by a relative error of at most 0.02.
Values may be sent and summed in bfloat16 or wider, within the bound.
A program may use at most 128 MiB of HBM per device.

v0:
```python
import jax
import jax.numpy as jnp
from jax import lax
from jax.sharding import PartitionSpec as P

BLOCK = 128
HIGHEST = lax.Precision.HIGHEST


def prefix(part, axis, combine, identity):
    place = lax.axis_index(axis)
    gathered = lax.all_gather(part, axis)
    state = jnp.zeros_like(part) + jnp.asarray(identity, part.dtype)

    def one(step, state):
        return combine(state, lax.dynamic_index_in_dim(gathered, step, 0, False))

    return lax.fori_loop(0, place, one, state)


def top_bit(differ, bit_count):
    result = jnp.zeros_like(differ)
    for shift in range(1, bit_count):
        result = result + (jnp.right_shift(differ, shift) > 0).astype(jnp.int32)
    return result


def split_pair(wide):
    upper_part = wide.astype(jnp.bfloat16)
    lower_part = (wide - upper_part.astype(jnp.float32)).astype(jnp.bfloat16)
    return (upper_part, lower_part)


def body(tokens, log_decay, w_query, w_key, w_value, w_level, w_out):
    rows = tokens.shape[0]
    heads_local = log_decay.shape[1]
    head_size = w_out.shape[0] // heads_local
    level_count = w_level.shape[1] // heads_local
    kv_local = w_key.shape[1] // head_size
    group_size = heads_local // kv_local
    matrices = (w_query, w_key, w_value, w_level)
    piece = lax.all_gather(tokens, "tp", axis=1, tiled=True)
    sums = tuple(
        (jnp.dot(piece, matrix, preferred_element_type=jnp.float32) for matrix in matrices)
    )
    query = sums[0].astype(jnp.bfloat16).reshape(rows, kv_local, group_size, head_size)
    keys_here = sums[1].astype(jnp.bfloat16).reshape(rows, kv_local, head_size)
    values_here = sums[2].astype(jnp.bfloat16).reshape(rows, kv_local, head_size)
    level_weight = jax.nn.softplus(sums[3]).reshape(rows, heads_local, level_count)
    decay_sum = jnp.cumsum(log_decay, axis=0)
    slab_total = decay_sum[rows - 1]
    before = prefix(slab_total, "seq", jnp.add, jnp.zeros_like(slab_total))
    ends_here = before + slab_total
    positions = jnp.arange(rows, dtype=jnp.int32)
    block_of = positions // BLOCK
    local_bits = (rows // BLOCK).bit_length() - 1
    block_differ = jnp.bitwise_xor(block_of[:, None], block_of[None, :])
    level_table = jnp.where(block_differ == 0, 0, 1 + top_bit(block_differ, local_bits))
    causal = positions[:, None] >= positions[None, :]
    decay_heads = decay_sum.T
    gaps = jnp.where(causal[None], decay_heads[:, :, None] - decay_heads[:, None, :], -jnp.inf)
    picked = jnp.zeros((heads_local, rows, rows), jnp.float32)
    for level in range(local_bits + 1):
        picked = picked + jnp.where(
            level_table[None] == level, level_weight[:, :, level].T[:, :, None], 0.0
        )
    scores = jnp.einsum(
        "tgqd,sgd->gqts", query, keys_here, preferred_element_type=jnp.float32
    ).reshape(heads_local, rows, rows)
    mixing = (picked * jnp.exp(gaps) * scores).reshape(kv_local, group_size, rows, rows)
    mixing_upper, mixing_lower = split_pair(mixing)
    local_part = jnp.einsum(
        "gqts,sgd->gqtd", mixing_upper, values_here, preferred_element_type=jnp.float32
    )
    local_part = local_part + jnp.einsum(
        "gqts,sgd->gqtd", mixing_lower, values_here, preferred_element_type=jnp.float32
    )
    local_part = local_part.reshape(heads_local, rows, head_size)
    keep_factor = jnp.exp(slab_total[None, :] - decay_sum).reshape(rows, kv_local, group_size)
    weighted_keys = keep_factor[:, :, :, None] * keys_here.astype(jnp.float32)[:, :, None, :]
    keys_upper, keys_lower = split_pair(weighted_keys)
    own_state = jnp.einsum(
        "tgqd,tge->gqde", keys_upper, values_here, preferred_element_type=jnp.float32
    )
    own_state = own_state + jnp.einsum(
        "tgqd,tge->gqde", keys_lower, values_here, preferred_element_type=jnp.float32
    )
    own_state = own_state.reshape(heads_local, head_size, head_size)
    seq_bits = lax.axis_size("seq").bit_length() - 1
    device = lax.axis_index("seq")
    empty = jnp.zeros((seq_bits, heads_local, head_size, head_size), jnp.float32)
    states = lax.all_gather(own_state[None], "seq", axis=0, tiled=True)
    slab_ends = lax.all_gather(ends_here[None], "seq", axis=0, tiled=True)
    sources = jnp.arange(states.shape[0], dtype=jnp.int32)
    earlier = sources < device
    highest_bit = top_bit(jnp.bitwise_xor(sources, device), seq_bits)
    onehot = jnp.logical_and(
        highest_bit[:, None] == jnp.arange(seq_bits, dtype=jnp.int32)[None, :], earlier[:, None]
    ).astype(jnp.float32)
    fading = jnp.exp(jnp.where(earlier[:, None], before[None, :] - slab_ends, -jnp.inf))
    buckets = empty + jnp.einsum("nb,nh,nhde->bhde", onehot, fading, states, precision=HIGHEST)
    query_heads = query.reshape(rows, heads_local, head_size)
    buckets_upper, buckets_lower = split_pair(buckets)
    per_level = jnp.einsum(
        "thd,bhde->bthe", query_heads, buckets_upper, preferred_element_type=jnp.float32
    )
    per_level = per_level + jnp.einsum(
        "thd,bhde->bthe", query_heads, buckets_lower, preferred_element_type=jnp.float32
    )
    span_weight = (
        level_weight[:, :, local_bits + 1 : local_bits + 1 + seq_bits]
        * jnp.exp(decay_sum)[:, :, None]
    )
    remote_part = jnp.einsum("bthe,thb->hte", per_level, span_weight, precision=HIGHEST)
    combined = local_part + remote_part
    normed = (
        combined * lax.rsqrt(jnp.mean(combined * combined, axis=-1, keepdims=True) + 1e-05)
    ).astype(jnp.bfloat16)
    partial_out = jnp.einsum(
        "htd,hde->te",
        normed,
        w_out.reshape(heads_local, head_size, w_out.shape[1]),
        preferred_element_type=jnp.float32,
    )
    return lax.psum_scatter(partial_out.astype(jnp.bfloat16), "tp", scatter_dimension=1, tiled=True)


def solution(mesh):
    in_specs = (
        P("seq", "tp"),
        P("seq", "tp"),
        P(None, "tp"),
        P(None, "tp"),
        P(None, "tp"),
        P(None, "tp"),
        P("tp", None),
    )
    out_specs = P("seq", "tp")
    return jax.shard_map(body, mesh=mesh, in_specs=in_specs, out_specs=out_specs, check_vma=False)
```

profile of v0, /device:TPU:1, one launch (start us, length us, event | category | flops | bytes accessed | tf_op | source)
XLA Modules:
  0.0 341.4 jit_solution(4485512293242226166)
XLA Ops:
  6.5 0.7 all-gather.6.cloned.1.call-update
  7.3 0.7 reshape.296
  8.0 1.2 reduce-window.6
  9.9 53.9 %all-gather.6.cloned.1.call-done = bf16[512,4096]{1,0:T(8,128)(2,1)} async-done(((bf16[512,1024]{1,0:T(8,128)(2,1)}), bf16[512,4096]{1,0:T(8,128)(2,1)}) %all-gather.6.cloned.1.call-update) | async-done | bytes 4194320 | tf_op jit(solution)/shard_map/all_gather | solution.py:42
  63.8 3.4 %convolution_convert_fusion.2 = bf16[512,128]{1,0:T(8,128)(2,1)S(1)} fusion(bf16[512,4096]{1,0:T(8,128)(2,1)} %all-gather.6.cloned.1.call-done, bf16[4096,128]{1,0:T(8,128)(2,1)S(1)} %copy-done), kind=kOutput, calls=%fused_computation.24 | convolution fusion | flops 536936448 | bytes 5373952 | tf_op jit(solution)/shard_map/dot_general | solution.py:44
  67.4 3.8 %fusion.14 = bf16[512,128,1]{1,0,2:T(8,128)(2,1)S(1)} fusion(bf16[512,4096]{1,0:T(8,128)(2,1)} %all-gather.6.cloned.1.call-done, bf16[4096,128]{1,0:T(8,128)(2,1)} %param.13), kind=kOutput, calls=%fused_computation.25 | convolution fusion | flops 536936448 | bytes 5373952 | tf_op jit(solution)/shard_map/dot_general | solution.py:44
  71.5 1.0 convolution_add_fusion
  73.9 41.7 %all-gather.2 = f32[64,1,4]{2,1,0:T(1,128)S(1)} all-gather(f32[1,1,4]{2,1,0:T(1,128)S(1)} %bitcast.109), channel_id=1, replica_groups=mesh['seq'=64,'tp'=4] {'seq'}, dimensions={0}, use_global_device_ids=true | all-gather | bytes 1040 | tf_op jit(solution)/shard_map/all_gather | solution.py:12
  115.8 124.5 %all-reduce = f32[256]{0:T(256)S(1)} all-reduce(f32[256]{0:T(256)S(1)} %add_dynamic-update-slice_fusion), channel_id=2, replica_groups=mesh['seq'=64,'tp'=4] {'seq'}, use_global_device_ids=true, to_apply=%add | all-reduce | flops 256 | bytes 2048
  240.5 0.8 iota_compare_fusion
  241.3 0.7 fusion.21
  242.0 3.6 %compare_select_fusion = f32[512,36]{0,1:T(8,128)S(1)} fusion(bf16[512,4096]{1,0:T(8,128)(2,1)} %all-gather.6.cloned.1.call-done, bf16[4096,36]{0,1:T(8,128)(2,1)S(1)} %copy-done.4), kind=kOutput, calls=%fused_computation.46 | convolution fusion | flops 151105536 | bytes 4562944 | tf_op jit(solution)/shard_map/dot_general | solution.py:44
  245.8 5.9 %convolution_convert_fusion = bf16[512,512]{0,1:T(8,128)(2,1)S(1)} fusion(bf16[512,4096]{1,0:T(8,128)(2,1)} %all-gather.6.cloned.1.call-done, bf16[4096,512]{1,0:T(8,128)(2,1)} %param.11), kind=kOutput, calls=%fused_computation.20 | convolution fusion | flops 2147745792 | bytes 8912896 | tf_op jit(solution)/shard_map/dot_general | solution.py:44
  251.6 2.6 bitcast_multiply_fusion.1
  254.2 1.9 copy-done.1
  256.2 0.7 fusion.4
  256.9 20.4 %fusion = f32[6,4,128,128]{3,0,2,1:T(8,128)S(1)} fusion(f32[64,4,128,128]{3,2,1,0:T(8,128)} %bitcast.101, f32[64,4]{0,1:T(4,128)S(1)} %select_exponential_fusion, s32[64]{0:T(128)S(1)} %fusion.45, pred[64]{0:T(512)(128)(4,1)S(1)} %iota_compare_fusion.2), kind=kOutput, calls=%fused_computation.2 | convolution fusion | flops 306184960 | bytes 18351424 | tf_op jit(solution)/shard_map/nb,nh,nhde->bhde/dot_general | solution.py:101
  277.3 1.0 fusion.23
  278.3 1.2 fusion.2
  279.5 1.0 copy-done.2
  280.5 0.9 multiply_reduce_fusion
  281.4 1.3 copy-done.3
  282.7 4.4 %bitcast_convert_fusion = bf16[512,4096]{1,0:T(8,128)(2,1)} fusion(bf16[4,128,4096]{2,1,0:T(8,128)(2,1)S(1)} %bitcast.102, f32[4,512,128]{1,2,0:T(8,128)S(1)} %get-tuple-element.48, f32[4,512]{1,0:T(4,128)S(1)} %add_rsqrt_fusion), kind=kOutput, calls=%fused_computation.3 | convolution fusion | flops 2150105088 | bytes 9445376 | tf_op jit(solution)/shard_map/htd,hde->te/dot_general | solution.py:119
  287.1 47.8 %reduce-scatter.2.cloned.1.call-done = bf16[512,1024]{1,0:T(8,128)(2,1)} async-done(((bf16[512,4096]{1,0:T(8,128)(2,1)}), bf16[512,1024]{1,0:T(8,128)(2,1)}) %reduce-scatter.2.cloned.1.call-update) | async-done | bytes 1048592 | tf_op jit(solution)/shard_map/reduce_scatter | solution.py:125
  (43 shorter events, 2.4 us)
Async XLA Ops:
  6.5 57.3 %copy-start = (bf16[4096,128]{1,0:T(8,128)(2,1)S(1)}, bf16[4096,128]{1,0:T(8,128)(2,1)}, u32[]{:S(2)}) copy-start(bf16[4096,128]{1,0:T(8,128)(2,1)} %param.12) | copy-start | bytes 3145732
  6.5 57.3 %all-gather.6.cloned.1.call-start = ((), (), s32[]{:S(2)}) async-start(), calls=%async_computation.1 | async-start | bytes 5242880 | tf_op jit(solution)/shard_map/all_gather | solution.py:42
  7.3 249.6 %all-gather.8.cloned.1.call-start = ((), (), s32[]{:S(2)}) async-start(), calls=%async_computation.3 | async-start | bytes 17039360 | tf_op jit(solution)/shard_map/all_gather | solution.py:92
  67.3 5.3 %copy-start.6 = (u32[256]{0:T(256)S(1)}, u32[256]{0:T(256)}, u32[]{:S(2)}) copy-start(u32[256]{0:T(256)} %constant.67) | copy-start | bytes 3076
  67.4 174.6 %copy-start.4 = (bf16[4096,36]{0,1:T(8,128)(2,1)S(1)}, bf16[4096,36]{0,1:T(8,128)(2,1)}, u32[]{:S(2)}) copy-start(bf16[4096,36]{0,1:T(8,128)(2,1)} %param.14) | copy-start | bytes 884740
  72.5 262.3 %reduce-scatter.2.cloned.1.call-start = ((), (), s32[]{:S(2)}) async-start(), calls=%async_computation.2 | async-start | bytes 5242880 | tf_op jit(solution)/shard_map/reduce_scatter | solution.py:125
  245.7 5.9 %copy-start.5 = (pred[512,512]{0,1:T(8,128)(4,1)S(1)}, pred[512,512]{0,1:T(8,128)(4,1)}, u32[]{:S(2)}) copy-start(pred[512,512]{0,1:T(8,128)(4,1)} %iota_compare_fusion) | copy-start | bytes 786436
  254.2 1.9 copy-start.1
  278.3 2.2 copy-start.2
  280.5 2.2 copy-start.3
Sparse Core Ops, SparseCore 0:
  9.2 54.6 all-gather.5
  72.7 100.9 all-gather.7
  287.2 47.6 reduce-scatter.1
where the time goes:
time: 342 us; the launch traced here: 341 us
  blocking collectives  166 us (49%)
  waiting for transfers between devices  102 us (30%)
  matrix products  49.1 us (14%)
  between operations  14 us (4%)
  local copies, waits for them, and re-layouts  6.27 us (2%)
    unnamed x1, blocking collectives  124 us
    all_gather x1, waiting for transfers between devices, body(): piece = lax.all_gather(tokens, 'tp', axis=1, tiled=True)  53.9 us
    reduce_scatter x1, waiting for transfers between devices, body(): lax.psum_scatter(partial_out.astype(jnp.bfloat16), 'tp', scatter_dimensio...  47.8 us
    all_gather x1, blocking collectives, prefix(): gathered = lax.all_gather(part, axis)  41.7 us
    dot_general x1, matrix products, body(): jnp.einsum('nb,nh,nhde->bhde', onehot, fading, states, precision=HIGHEST)  20.4 us
    dot_general x4, matrix products, body(): jnp.dot(piece, matrix, preferred_element_type=jnp.float32)  16.7 us
  transfers between devices with their start and end apart: 3, of which 2 were waited for; matrix products, arithmetic and copies ran while one was open for 5% of the time, Pallas kernels for 0%

commit v1 on v0

--- a/solution.py
+++ b/solution.py
@@ -5,6 +5,23 @@
 
 BLOCK = 128
 HIGHEST = lax.Precision.HIGHEST
+
+
+def in_order(blocks, dim):
+    blocks = jnp.moveaxis(blocks, 0, dim)
+    dims = blocks.shape
+    return blocks.reshape(*dims[:dim], dims[dim] * dims[dim + 1], *dims[dim + 2 :])
+
+
+def collected_by_bits(x, axis):
+    peers, index = (lax.axis_size(axis), lax.axis_index(axis))
+    blocks, bit = (x[None], 1)
+    while bit < peers:
+        other = lax.ppermute(blocks, axis, [(i, i ^ bit) for i in range(peers)])
+        low = index & bit == 0
+        blocks = jnp.concatenate([jnp.where(low, blocks, other), jnp.where(low, other, blocks)])
+        bit *= 2
+    return blocks
 
 
 def prefix(part, axis, combine, identity):
@@ -39,7 +56,7 @@
     kv_local = w_key.shape[1] // head_size
     group_size = heads_local // kv_local
     matrices = (w_query, w_key, w_value, w_level)
-    piece = lax.all_gather(tokens, "tp", axis=1, tiled=True)
+    piece = in_order(collected_by_bits(tokens, "tp"), 1)
     sums = tuple(
         (jnp.dot(piece, matrix, preferred_element_type=jnp.float32) for matrix in matrices)
     )

time: 342 us -> 364 us (1.064)
  waiting for transfers between devices: 102 us -> 113 us
  starting transfers between devices: 0.08 us -> 6.37 us
  matrix products: 49.1 us -> 43.9 us
  other arithmetic: 3.27 us -> 8.29 us
  blocking collectives: 166 us -> 170 us
    ppermute x0 -> x2, waiting for transfers between devices: none -> 64.2 us  [collected_by_bits(): other = lax.ppermute(blocks, axis, [(i, i ^ bit) for i in range(peers)])]
    all_gather x1 -> x0, waiting for transfers between devices: 53.9 us -> none  [body(): piece = lax.all_gather(tokens, 'tp', axis=1, tiled=True)]
    ppermute x0 -> x2, starting transfers between devices: none -> 6.33 us  [collected_by_bits(): other = lax.ppermute(blocks, axis, [(i, i ^ bit) for i in range(peers)])]
    dot_general x4, matrix products: 16.7 us -> 11.5 us  [body(): jnp.dot(piece, matrix, preferred_element_type=jnp.float32)]
    select_n x0 -> x2, other arithmetic: none -> 3.81 us  [collected_by_bits(): jnp.where(low, blocks, other)]
  transfers between devices with their start and end apart: 3 -> 4, of which waited for: 2 -> 3; matrix products, arithmetic and copies ran while one was open for 5% -> 4% of each run, Pallas kernels for 0% -> 0%
where the time goes in v1:
time: 364 us
  blocking collectives  170 us (47%)
  waiting for transfers between devices  113 us (31%)
  matrix products  43.9 us (12%)
  between operations  14.3 us (4%)
  other arithmetic  8.29 us (2%)
  local copies, waits for them, and re-layouts  7.91 us (2%)
  starting transfers between devices  6.37 us (2%)
    unnamed x1, blocking collectives  125 us
    ppermute x2, waiting for transfers between devices, collected_by_bits(): other = lax.ppermute(blocks, axis, [(i, i ^ bit) for i in range(peers)])  64.2 us
    reduce_scatter x1, waiting for transfers between devices, body(): lax.psum_scatter(partial_out.astype(jnp.bfloat16), 'tp', scatter_dimensio...  48.9 us
    all_gather x1, blocking collectives, prefix(): gathered = lax.all_gather(part, axis)  44.9 us
    dot_general x1, matrix products, body(): jnp.einsum('nb,nh,nhde->bhde', onehot, fading, states, precision=HIGHEST)  20.5 us
    dot_general x4, matrix products, body(): jnp.dot(piece, matrix, preferred_element_type=jnp.float32)  11.5 us
  transfers between devices with their start and end apart: 4, of which 3 were waited for; matrix products, arithmetic and copies ran while one was open for 4% of the time, Pallas kernels for 0%

profile of v1, /device:TPU:1, one launch (start us, length us, event | category | flops | bytes accessed | tf_op | source)
XLA Modules:
  0.0 363.6 jit_solution(5326039434960570081)
XLA Ops:
  6.5 1.6 copy.65
  8.1 2.2 collective-permute-start
  10.4 21.6 %collective-permute-done = bf16[1,512,1024]{1,2,0:T(8,128)(2,1)} collective-permute-done((bf16[1,512,1024]{1,2,0:T(8,128)(2,1)S(1)}, bf16[1,512,1024]{1,2,0:T(8,128)(2,1)}, u32[]{:S(2)}, u32[]{:S(2)}) %collective-permute-start) | collective-permute-done | bytes 1048608 | tf_op jit(solution)/shard_map/ppermute | solution.py:20
  32.0 1.7 broadcast_select_fusion.3
  33.7 1.5 pad_maximum_fusion.1
  35.2 4.1 %collective-permute-start.1 = (bf16[2,512,1024]{1,2,0:T(8,128)(2,1)}, bf16[2,512,1024]{1,2,0:T(8,128)(2,1)}, u32[]{:S(2)}, u32[]{:S(2)}) collective-permute-start(bf16[2,512,1024]{1,2,0:T(8,128)(2,1)} %pad_maximum_fusion.1), channel_id=1, source_target_pairs={{0,2},{1,3},{2,0},{3,1},{4,6},{5,7},{6,4},{7,5},{8,10},{9,11},{10,... | collective-permute-start | bytes 6291464 | tf_op jit(solution)/shard_map/ppermute | solution.py:20
  39.3 1.2 reduce-window.6
  41.2 42.6 %collective-permute-done.1 = bf16[2,512,1024]{1,2,0:T(8,128)(2,1)} collective-permute-done((bf16[2,512,1024]{1,2,0:T(8,128)(2,1)}, bf16[2,512,1024]{1,2,0:T(8,128)(2,1)}, u32[]{:S(2)}, u32[]{:S(2)}) %collective-permute-start.1) | collective-permute-done | bytes 2097184 | tf_op jit(solution)/shard_map/ppermute | solution.py:20
  83.8 2.1 broadcast_select_fusion.1
  86.4 1.3 fusion.14
  88.4 1.3 convolution_convert_fusion.2
  92.4 44.9 %all-gather.2 = f32[64,1,4]{2,1,0:T(1,128)S(1)} all-gather(f32[1,1,4]{2,1,0:T(1,128)S(1)} %bitcast.120), channel_id=1, replica_groups=mesh['seq'=64,'tp'=4] {'seq'}, dimensions={0}, use_global_device_ids=true | all-gather | bytes 1040 | tf_op jit(solution)/shard_map/all_gather | solution.py:29
  137.5 124.7 %all-reduce = f32[256]{0:T(256)S(1)} all-reduce(f32[256]{0:T(256)S(1)} %add_dynamic-update-slice_fusion), channel_id=2, replica_groups=mesh['seq'=64,'tp'=4] {'seq'}, use_global_device_ids=true, to_apply=%add | all-reduce | flops 256 | bytes 2048
  263.3 3.0 compare_select_fusion
  266.4 5.8 %convolution_convert_fusion = bf16[512,512]{0,1:T(8,128)(2,1)S(1)} fusion(bf16[512,4096]{0,1:T(8,128)(2,1)} %bitcast.111, bf16[4096,512]{1,0:T(8,128)(2,1)} %param.11), kind=kOutput, calls=%fused_computation.24 | convolution fusion | flops 2147745792 | bytes 8912896 | tf_op jit(solution)/shard_map/dot_general | solution.py:61
  272.3 2.6 bitcast_multiply_fusion.1
  274.9 1.9 copy-done.3
  277.6 20.5 %fusion = f32[6,4,128,128]{3,0,2,1:T(8,128)S(1)} fusion(f32[64,4,128,128]{3,2,1,0:T(8,128)} %bitcast.107, f32[64,4]{0,1:T(4,128)S(1)} %select_exponential_fusion, s32[64]{0:T(128)S(1)} %fusion.45, pred[64]{0:T(512)(128)(4,1)S(1)} %iota_compare_fusion.2), kind=kOutput, calls=%fused_computation.2 | convolution fusion | flops 306184960 | bytes 18351424 | tf_op jit(solution)/shard_map/nb,nh,nhde->bhde/dot_general | solution.py:118
  298.1 1.0 fusion.23
  299.1 1.1 fusion.2
  300.2 1.1 copy-done.4
  302.2 1.3 copy-done.6
  303.5 4.3 %bitcast_convert_fusion = bf16[512,4096]{1,0:T(8,128)(2,1)} fusion(bf16[4,128,4096]{2,1,0:T(8,128)(2,1)S(1)} %bitcast.113, f32[4,512,128]{1,2,0:T(8,128)S(1)} %get-tuple-element.52, f32[4,512]{1,0:T(4,128)S(1)} %add_rsqrt_fusion), kind=kOutput, calls=%fused_computation.3 | convolution fusion | flops 2150105088 | bytes 9445376 | tf_op jit(solution)/shard_map/htd,hde->te/dot_general | solution.py:136
  307.9 48.9 %reduce-scatter.2.cloned.1.call-done = bf16[512,1024]{1,0:T(8,128)(2,1)} async-done(((bf16[512,4096]{1,0:T(8,128)(2,1)}), bf16[512,1024]{1,0:T(8,128)(2,1)}) %reduce-scatter.2.cloned.1.call-update) | async-done | bytes 1048592 | tf_op jit(solution)/shard_map/reduce_scatter | solution.py:142
  (57 shorter events, 6.8 us)
Async XLA Ops:
  6.5 79.8 %copy-start = (bf16[4096,128]{1,0:T(8,128)(2,1)S(1)}, bf16[4096,128]{1,0:T(8,128)(2,1)}, u32[]{:S(2)}) copy-start(bf16[4096,128]{1,0:T(8,128)(2,1)} %param.13) | copy-start | bytes 3145732
  6.5 271.1 %all-gather.5.cloned.1.call-start = ((), (), s32[]{:S(2)}) async-start(), calls=%async_computation.2 | async-start | bytes 17039360 | tf_op jit(solution)/shard_map/all_gather | solution.py:109
  8.1 2.2 copy-start.5
  8.1 23.8 %collective-permute-start = (bf16[1,512,1024]{1,2,0:T(8,128)(2,1)S(1)}, bf16[1,512,1024]{1,2,0:T(8,128)(2,1)}, u32[]{:S(2)}, u32[]{:S(2)}) collective-permute-start(bf16[1,512,1024]{1,2,0:T(8,128)(2,1)S(1)} %bitcast.112), channel_id=1, source_target_pairs={{0,1},{1,0},{2,3},{3,2},{4,5},{5,4},{6,7},{7,6},{8,9},{9,8},{10,11... | collective-permute-start | bytes 3145736 | tf_op jit(solution)/shard_map/ppermute | solution.py:20
  10.4 28.9 %copy-start.8 = (f32[512,4]{0,1:T(4,128)S(1)}, f32[512,4]{0,1:T(4,128)}, u32[]{:S(2)}) copy-start(f32[512,4]{0,1:T(4,128)} %param.10) | copy-start | bytes 24580
  35.2 48.7 %collective-permute-start.1 = (bf16[2,512,1024]{1,2,0:T(8,128)(2,1)}, bf16[2,512,1024]{1,2,0:T(8,128)(2,1)}, u32[]{:S(2)}, u32[]{:S(2)}) collective-permute-start(bf16[2,512,1024]{1,2,0:T(8,128)(2,1)} %pad_maximum_fusion.1), channel_id=1, source_target_pairs={{0,2},{1,3},{2,0},{3,1},{4,6},{5,7},{6,4},{7,5},{8,10},{9,11},{10,... | collective-permute-start | bytes 6291464 | tf_op jit(solution)/shard_map/ppermute | solution.py:20
  86.3 1.9 copy-start.2
  86.4 2.0 copy-start.9
  88.4 2.8 copy-start.10
  88.4 174.9 %copy-start.7 = (bf16[4096,36]{0,1:T(8,128)(2,1)S(1)}, bf16[4096,36]{0,1:T(8,128)(2,1)}, u32[]{:S(2)}) copy-start(bf16[4096,36]{0,1:T(8,128)(2,1)} %param.14) | copy-start | bytes 884740
  91.1 265.6 %reduce-scatter.2.cloned.1.call-start = ((), (), s32[]{:S(2)}) async-start(), calls=%async_computation.1 | async-start | bytes 5242880 | tf_op jit(solution)/shard_map/reduce_scatter | solution.py:142
  274.9 1.9 copy-start.3
  299.1 2.2 copy-start.4
  301.3 2.2 copy-start.6
  303.5 53.2 %copy-start.1 = (bf16[4096,128]{1,0:T(8,128)(2,1)S(1)}, bf16[4096,128]{1,0:T(8,128)(2,1)}, u32[]{:S(2)}) copy-start(bf16[4096,128]{1,0:T(8,128)(2,1)} %param.13) | copy-start | bytes 3145732
Sparse Core Ops, SparseCore 0:
  91.3 105.4 all-gather.4
  308.0 48.6 reduce-scatter.1
